TPU v7x, 32 devices: a whole 2x2x4 slice. The times are simulated.
32 devices in a mesh: dp: 2 (over x), space: 16 (over z, y, core).
Axes of the slice: x: 2, y: 2, z: 4, core: 2. Of those that a mesh axis runs over, the one named last changes fastest.
Arguments:
- fields: bfloat16 [2, 64, 32, 32, 128], P('dp', 'space'), may hold values from -6 to 6
- cotangent: bfloat16 [2, 64, 32, 32, 128], P('dp', 'space'), may hold values from -6 to 6
- w_first: bfloat16 [3, 3, 128, 128], replicated, may hold values from -0.1875 to 0.1875
- w_second: bfloat16 [3, 3, 128, 128], replicated, may hold values from -0.1875 to 0.1875
- tile_links: int32 [64, 4, 5], P('space'), may hold values from 0 to 63, as said below
Outputs:
- mixed: bfloat16 [2, 64, 32, 32, 128], P('dp', 'space')
- grad_first: float32 [3, 3, 128, 128], replicated
- grad_second: float32 [3, 3, 128, 128], replicated
Inputs may be any that keep to these rules, and one draw needn't show every extreme that they name: `tile_links`: columns 0 and 3 are tile numbers; columns 1 and 4 are an edge or corner 0 to 3; column 2 is 0 or 1. The links are mutual: if side k of tile t reads edge e of tile u with flag f, side e of u reads edge k of t with flag f; if corner k of t reads corner q of u, corner q of u reads corner k of t. Tiles 4 * d to 4 * d + 3 lie on index d of space; every source of a tile lies on its index, the next or the previous one, the last index being next to the first. Only the first 4 tiles of an index read from the previous index and only the last 4 from the next, each through exactly one side and the two corners at that side's ends; each tile read there is read through a side by exactly one tile of the reading index, and the corners read from it are the ends of that edge.
All inputs are finite; a program needn't handle non-finite values.
Results may differ from a plain program's by a relative error of at most 0.0031.
Values may be sent and summed in bfloat16 or wider, within the bound.
A program may use at most 64 MiB of HBM per device.

v0:
```python
import functools

import jax
import jax.numpy as jnp
from jax import lax
from jax.experimental import pallas as pl
from jax.experimental.pallas import tpu as pltpu
from jax.sharding import PartitionSpec as P

F32 = jnp.float32
BF16 = jnp.bfloat16
MESH = pl.DeviceIdType.MESH
TRAVEL = (F32, F32, F32, F32)


def plan(dp_size, space_size, rows):
    mid = 2 if space_size % 4 == 0 else 1
    group = dp_size * mid
    far = space_size // (2 * mid)
    piece = -(-rows // (2 * group * 16)) * 16
    return mid, group, far, piece


def kernel(
    dp_size, space_size, tiles, side, chans, scale,
    links, f_ref, c_ref, w1_ref, w2_ref,
    mixed_ref, g1_ref, g2_ref,
    xc, ac, cc, gc, wb, deriv, agrad, rims, rim_corners,
    pool0, pool1, pool2, land0, land1, land2, out0, out1, out2,
    acc1, acc2, ra1, ra2, half1, half2, sb1, sb2, rb1, rb2, sc1, sc2, rc1, rc2, fo1, fo2,
    halo_send, halo_recv, red_send, red_recv,
):
    T, S, C = tiles, side, chans
    K = 3 * C
    pix = S * S
    pad_rows = S + 2
    su = S // 16
    own_units = 4 * T * su + T
    msg_units = T * su + T
    mid, group, far, piece = plan(dp_size, space_size, 9 * C)
    d = lax.axis_index("dp")
    s = lax.axis_index("space")
    core = lax.rem(s, 2)
    y = lax.rem(lax.div(s, 2), mid)
    z = lax.div(s, 2 * mid)
    b = d * mid + y
    lower = lax.rem(s + space_size - 1, space_size)
    upper = lax.rem(s + 1, space_size)
    partner = s + 1 - 2 * core

    def plane_peer(step):
        other = lax.rem(b + step, group)
        return (lax.div(other, mid), z * (2 * mid) + lax.rem(other, mid) * 2 + core)

    def far_peer(step):
        other = lax.rem(z + step, far)
        return (d, (other * mid + y) * 2 + core)

    barrier = pltpu.get_barrier_semaphore()
    greeted = [(d, lower), (d, upper), (d, partner)]
    greeted += [plane_peer(step) for step in range(1, group)]
    greeted += [far_peer(step) for step in range(1, far)]
    for peer in greeted:
        pl.semaphore_signal(barrier, inc=1, device_id=peer, device_id_type=MESH)

    def where_is(source):
        rel = lax.rem(lax.div(source, T) - s + 1 + space_size, space_size)
        return rel, lax.rem(source, T)

    strip_at, corner_at, face_lower, face_upper = {}, {}, [], []
    for t in range(T):
        low, up = 0, 0
        for k in range(4):
            rel, slot = where_is(links[t, k, 0])
            strip_at[t, k] = jnp.where(
                rel == 1,
                (slot * 4 + links[t, k, 1]) * su,
                jnp.where(rel == 0, own_units, own_units + msg_units) + slot * su,
            )
            low = low + jnp.where(rel == 0, k, 0)
            up = up + jnp.where(rel == 2, k, 0)
            rel, slot = where_is(links[t, k, 3])
            corner_at[t, k] = slot + jnp.where(
                rel == 1,
                4 * T * su,
                jnp.where(rel == 0, own_units, own_units + msg_units) + T * su,
            )
        face_lower.append(low)
        face_upper.append(up)

    row_id = lax.broadcasted_iota(jnp.int32, (S, S), 0)
    col_id = lax.broadcasted_iota(jnp.int32, (S, S), 1)
    same = (row_id == col_id).astype(F32)
    turned = (row_id + col_id == S - 1).astype(F32)
    unit_row = lax.broadcasted_iota(jnp.int32, (16, C), 0)
    line_row = lax.broadcasted_iota(jnp.int32, (S, C), 0)
    block_col = lax.broadcasted_iota(jnp.int32, (S, S, C), 1)

    pools, lands, outs = (pool0, pool1, pool2), (land0, land1, land2), (out0, out1, out2)

    def keep_strip(pool, t, k, strip):
        pool[pl.ds((t * 4 + k) * su, su)] = strip.astype(BF16).reshape(su, 16, C)

    def keep_corners(pool, t, corners):
        unit = jnp.zeros((16, C), F32)
        for k in range(4):
            unit = jnp.where(unit_row == k, corners[k], unit)
        pool[4 * T * su + t] = unit.astype(BF16)

    def keep_edges(pool, t, value):
        top, bottom = value[0], value[S - 1]
        keep_strip(pool, t, 0, top)
        keep_strip(pool, t, 1, value[:, S - 1, :])
        keep_strip(pool, t, 2, bottom)
        keep_strip(pool, t, 3, value[:, 0, :])
        keep_corners(pool, t, [top[0:1], top[S - 1 : S], bottom[S - 1 : S], bottom[0:1]])

    def halo_copies(which):
        copies = []
        for way, (peer, place) in enumerate(((lower, 1), (upper, 0))):
            copies.append(
                pltpu.make_async_remote_copy(
                    src_ref=outs[which].at[way],
                    dst_ref=lands[which].at[place],
                    send_sem=halo_send.at[which, way],
                    recv_sem=halo_recv.at[which, way],
                    device_id=(d, peer),
                    device_id_type=MESH,
                )
            )
        return copies

    def send_halo(which):
        pool, out = pools[which], outs[which]
        for way, faces in enumerate((face_lower, face_upper)):
            for t in range(T):
                out[way, pl.ds(t * su, su)] = pool[pl.ds((t * 4 + faces[t]) * su, su)]
                out[way, T * su + t] = pool[4 * T * su + t]

    def take_halo(which, copies):
        pool = pools[which]
        for copy in copies:
            copy.wait_recv()
        for place in range(2):
            pool[pl.ds(own_units + place * msg_units, msg_units)] = lands[which][place]
        for t in range(T):
            for k in range(4):
                strip = pool[pl.ds(strip_at[t, k], su)].reshape(S, C)
                flag = links[t, k, 2].astype(F32)
                turn = (flag * turned + (1.0 - flag) * same).astype(BF16)
                rims[t, k] = jnp.dot(turn, strip, preferred_element_type=F32)
                unit = pool[corner_at[t, k]].astype(F32)
                rim_corners[t, k] = jnp.broadcast_to(
                    jnp.sum(jnp.where(unit_row == links[t, k, 4], unit, 0.0), 0, keepdims=True),
                    (8, C),
                )

    def shifted(dst, t, at, value, left, right, columns):
        extent = columns.ndim - 2
        last = S - 1
        before = jnp.where(columns == 0, left, pltpu.roll(value, 1, axis=extent))
        after = jnp.where(columns == last, right, pltpu.roll(value, last, axis=extent))
        dst[t, at, :, 0:C] = before.astype(BF16)
        dst[t, at, :, C : 2 * C] = value.astype(BF16)
        dst[t, at, :, 2 * C : K] = after.astype(BF16)

    def fill_padded(dst, t, value):
        left, right = rims[t, 3], rims[t, 1]
        shifted(dst, t, pl.ds(1, S), value, left[:, None, :], right[:, None, :], block_col)
        tl, tr = rim_corners[t, 0, 0:1], rim_corners[t, 1, 0:1]
        br, bl = rim_corners[t, 2, 0:1], rim_corners[t, 3, 0:1]
        shifted(dst, t, 0, rims[t, 0], tl, tr, line_row)
        shifted(dst, t, S + 1, rims[t, 2], bl, br, line_row)

    def conv(src, t, kernel_rows, order):
        lhs = jnp.concatenate([src[t, r : r + S].reshape(pix, K) for r in order], axis=1)
        return jnp.dot(lhs, kernel_rows, preferred_element_type=F32)

    def lower_rows(t, value):
        zero = jnp.zeros((1, S, C), BF16)
        for r in range(3):
            lanes = slice(r * C, (r + 1) * C)
            gc[t, r : r + S, :, lanes] = value
            for at in range(r):
                gc[t, at : at + 1, :, lanes] = zero
            for at in range(r + S, pad_rows):
                gc[t, at : at + 1, :, lanes] = zero

    def kernel_grad(padded, acc):
        total = None
        for t in range(T):
            part = lax.dot_general(
                padded[t].reshape(pad_rows * S, K),
                gc[t].reshape(pad_rows * S, K),
                (((0,), (0,)), ((), ())),
                preferred_element_type=F32,
            )
            total = part if total is None else total + part
        for r in range(3):
            for c in range(3):
                acc[pl.ds((r * 3 + c) * C, C)] = total[c * C : (c + 1) * C, r * C : (r + 1) * C]
        if 2 * group * piece > 9 * C:
            acc[9 * C :] = jnp.zeros((2 * group * piece - 9 * C, C), F32)

    half_rows = group * piece
    stage_at = (0, 1, group, group + far - 1, 2 * group + far - 2)

    def remote(which, index, src, dst, peer):
        return pltpu.make_async_remote_copy(
            src_ref=src, dst_ref=dst,
            send_sem=red_send.at[which, index], recv_sem=red_recv.at[which, index],
            device_id=peer, device_id_type=MESH,
        )

    accs, ras, halves = (acc1, acc2), (ra1, ra2), (half1, half2)
    sbs, rbs, scs, rcs, fos = (sb1, sb2), (rb1, rb2), (sc1, sc2), (rc1, rc2), (fo1, fo2)
    pending = []

    def launch(copies):
        for copy in copies:
            copy.start()
        pending.extend(copies)
        return copies

    def landed(copies):
        for copy in copies:
            copy.wait_recv()

    def pair_start(g):
        src = accs[g].at[pl.ds((1 - core) * half_rows, half_rows)]
        return launch([remote(g, 0, src, ras[g], (d, partner))])

    def plane_start(g, copies):
        landed(copies)
        halves[g][...] = accs[g][pl.ds(core * half_rows, half_rows)] + ras[g][...]
        result = []
        for step in range(1, group):
            other = lax.rem(b + step, group)
            sbs[g][step - 1] = halves[g][pl.ds(other * piece, piece)].astype(sbs[g].dtype)
            result.append(
                remote(g, stage_at[1] + step - 1, sbs[g].at[step - 1], rbs[g].at[step - 1], plane_peer(step))
            )
        return launch(result)

    def far_start(g, copies):
        landed(copies)
        total = halves[g][pl.ds(b * piece, piece)]
        for step in range(1, group):
            total = total + rbs[g][step - 1].astype(F32)
        scs[g][...] = total.astype(scs[g].dtype)
        return launch([
            remote(g, stage_at[2] + step - 1, scs[g], rcs[g].at[z], far_peer(step))
            for step in range(1, far)
        ])

    def back_start(g, copies):
        landed(copies)
        total = jnp.zeros((piece, C), F32)
        mine = scs[g][...].astype(F32)
        for at in range(far):
            total = total + jnp.where(z == at, mine, rcs[g][at].astype(F32))
        fos[g][core, b] = (total * scale).astype(fos[g].dtype)
        spot = fos[g].at[core, b]
        return launch([
            remote(g, stage_at[3] + step - 1, spot, spot, plane_peer(step))
            for step in range(1, group)
        ])

    def pair_back(g, copies):
        landed(copies)
        spot = fos[g].at[core]
        return launch([remote(g, stage_at[4], spot, spot, (d, partner))])

    def finish(g, copies, out):
        landed(copies)
        out[...] = fos[g][...].reshape(2 * half_rows, C)[: 9 * C].astype(F32).reshape(3, 3, C, C)

    @pl.loop(0, T)
    def _(t):
        keep_edges(pool0, t, f_ref[0, t].astype(F32))

    send_halo(0)
    pl.semaphore_wait(barrier, len(greeted))
    copies0 = halo_copies(0)
    launch(copies0)

    for r in range(3):
        for c in range(3):
            wb[pl.ds((r * 3 + c) * C, C)] = w2_ref[r, c].astype(F32).T.astype(BF16)

    @pl.loop(0, T)
    def _(t):
        value = c_ref[0, t].astype(F32)
        blank = jnp.zeros((1, S, K), BF16)
        zero = jnp.zeros((), F32)
        up = jnp.where(block_col == S - 1, zero, pltpu.roll(value, S - 1, axis=1))
        down = jnp.where(block_col == 0, zero, pltpu.roll(value, 1, axis=1))
        cc[t, pl.ds(1, S), :, 0:C] = up.astype(BF16)
        cc[t, pl.ds(1, S), :, C : 2 * C] = c_ref[0, t]
        cc[t, pl.ds(1, S), :, 2 * C : K] = down.astype(BF16)
        cc[t, 0:1] = blank
        cc[t, S + 1 : S + 2] = blank
        top = jnp.dot(cc[t, 1], wb[0:K], preferred_element_type=F32)
        bottom = jnp.dot(cc[t, S], wb[2 * K : 3 * K], preferred_element_type=F32)
        corners = {}
        for column, c, k in ((0, 0, 3), (S - 1, 2, 1)):
            line = value[:, column, :].astype(BF16)
            parts = [
                jnp.dot(line, wb[(r * 3 + c) * C : (r * 3 + c + 1) * C], preferred_element_type=F32)
                for r in range(3)
            ]
            strip = parts[1]
            strip = strip + jnp.where(line_row == S - 1, 0.0, pltpu.roll(parts[0], S - 1, axis=0))
            strip = strip + jnp.where(line_row == 0, 0.0, pltpu.roll(parts[2], 1, axis=0))
            keep_strip(pool1, t, k, strip)
            corners[c] = (parts[0][0:1], parts[2][S - 1 : S])
        keep_strip(pool1, t, 0, top)
        keep_strip(pool1, t, 2, bottom)
        keep_corners(pool1, t, [corners[0][0], corners[2][0], corners[2][1], corners[0][1]])

    send_halo(1)
    copies1 = launch(halo_copies(1))

    @pl.loop(0, T)
    def _(t):
        agrad[t] = conv(cc, t, wb[...], (2, 1, 0)).reshape(S, S, C)

    take_halo(0, copies0)

    @pl.loop(0, T)
    def _(t):
        fill_padded(xc, t, f_ref[0, t].astype(F32))
        hidden = conv(xc, t, w1_ref[...].reshape(9 * C, C), (0, 1, 2))
        gate = jax.nn.sigmoid(hidden)
        active = (hidden * gate).reshape(S, S, C)
        deriv[t] = (gate * (1.0 + hidden * (1.0 - gate))).reshape(S, S, C)
        ac[t, pl.ds(1, S), :, C : 2 * C] = active.astype(BF16)
        keep_edges(pool2, t, active)

    send_halo(2)
    copies2 = launch(halo_copies(2))

    take_halo(1, copies1)

    @pl.loop(0, T)
    def _(t):
        agrad[t, 0] = agrad[t, 0] + rims[t, 0]
        agrad[t, S - 1] = agrad[t, S - 1] + rims[t, 2]
        for column, k, above, below in ((0, 3, 0, 3), (S - 1, 1, 1, 2)):
            strip = rims[t, k]
            strip = strip + jnp.where(line_row == 0, rim_corners[t, above, 0:1], 0.0)
            strip = strip + jnp.where(line_row == S - 1, rim_corners[t, below, 0:1], 0.0)
            agrad[t, :, column : column + 1, :] = (
                agrad[t, :, column : column + 1, :] + strip[:, None, :]
            )
        lower_rows(t, (agrad[t] * deriv[t]).astype(BF16))

    kernel_grad(xc, acc1)
    first = pair_start(0)

    take_halo(2, copies2)

    @pl.loop(0, T)
    def _(t):
        fill_padded(ac, t, ac[t, pl.ds(1, S), :, C : 2 * C].astype(F32))
        lower_rows(t, c_ref[0, t])

    first = plane_start(0, first)
    kernel_grad(ac, acc2)
    second = pair_start(1)
    first = far_start(0, first)

    def output(t):
        out = conv(ac, t, w2_ref[...].reshape(9 * C, C), (0, 1, 2)).reshape(S, S, C)
        mixed_ref[0, t] = (f_ref[0, t].astype(F32) + out).astype(BF16)

    pl.loop(0, T // 2)(output)
    second = plane_start(1, second)
    first = back_start(0, first)
    pl.loop(T // 2, T)(output)
    second = far_start(1, second)
    first = pair_back(0, first)
    second = back_start(1, second)
    finish(0, first, g1_ref)
    second = pair_back(1, second)
    finish(1, second, g2_ref)
    for copy in pending:
        copy.wait_send()


def block(mesh, fields, cotangent, w_first, w_second, tile_links):
    samples, T, S, _, C = fields.shape
    assert samples == 1
    dp_size, space_size = mesh.shape["dp"], mesh.shape["space"]
    mid, group, far, piece = plan(dp_size, space_size, 9 * C)
    scale = float(samples * dp_size * T * space_size * S * S) ** (-0.5)
    su = S // 16
    own_units, msg_units = 4 * T * su + T, T * su + T
    vmem = pltpu.VMEM
    padded = vmem((T, S + 2, S, 3 * C), BF16)
    twice = lambda shape, kind: [vmem(shape, kind), vmem(shape, kind)]
    stages = 2 * group + far - 1
    specs = pl.BlockSpec(memory_space=pltpu.VMEM)
    return pl.pallas_call(
        functools.partial(kernel, dp_size, space_size, T, S, C, scale),
        out_shape=(
            jax.ShapeDtypeStruct(fields.shape, BF16),
            jax.ShapeDtypeStruct(w_first.shape, F32),
            jax.ShapeDtypeStruct(w_second.shape, F32),
        ),
        in_specs=[pl.BlockSpec(memory_space=pltpu.SMEM), specs, specs, specs, specs],
        out_specs=(specs, specs, specs),
        scratch_shapes=[
            padded, padded, padded, padded,
            vmem((9 * C, C), BF16),
            vmem((T, S, S, C), F32),
            vmem((T, S, S, C), F32),
            vmem((T, 4, S, C), F32),
            vmem((T, 4, 8, C), F32),
        ]
        + [vmem((own_units + 2 * msg_units, 16, C), BF16)] * 3
        + [vmem((2, msg_units, 16, C), BF16)] * 6
        + twice((2 * group * piece, C), F32)
        + twice((group * piece, C), TRAVEL[0])
        + twice((group * piece, C), F32)
        + twice((group - 1, piece, C), TRAVEL[1])
        + twice((group - 1, piece, C), TRAVEL[1])
        + twice((piece, C), TRAVEL[2])
        + twice((far, piece, C), TRAVEL[2])
        + twice((2, group, piece, C), TRAVEL[3])
        + [
            pltpu.SemaphoreType.DMA((3, 2)),
            pltpu.SemaphoreType.DMA((3, 2)),
            pltpu.SemaphoreType.DMA((2, stages)),
            pltpu.SemaphoreType.DMA((2, stages)),
        ],
        compiler_params=pltpu.CompilerParams(
            collective_id=0, has_side_effects=True, vmem_limit_bytes=56 * 1024 * 1024
        ),
    )(tile_links, fields, cotangent, w_first, w_second)


def solution(mesh):
    placed = (
        P("dp", "space", None, None, None),
        P("dp", "space", None, None, None),
        P(),
        P(),
        P("space", None, None),
    )
    return jax.shard_map(
        functools.partial(block, mesh),
        mesh=mesh,
        in_specs=placed,
        out_specs=(P("dp", "space", None, None, None), P(), P()),
        check_vma=False,
    )
```

profile of v0, /device:TPU:0, one launch (start us, length us, event | category | flops | bytes accessed | tf_op | source)
XLA Modules:
  0.0 53.9 jit_solution(6266290422948654444)
XLA Ops:
  0.6 48.8 %shard_map.76 = (bf16[1,4,32,32,128]{4,3,2,1,0:T(8,128)(2,1)}, f32[3,3,128,128]{3,2,1,0:T(8,128)}, f32[3,3,128,128]{3,2,1,0:T(8,128)}) custom-call(s32[4,4,5]{2,1,0:T(4,128)} %links.1, bf16[1,4,32,32,128]{4,3,2,1,0:T(8,128)(2,1)} %f_ref.1, bf16[1,4,32,32,128]{4,3,2,1,0:T(8,128)(2,1)} %c_ref.1, bf16[3,3,128,128]{3,2,1,0:T(8,128)(2,1)} %w1_ref.1, ...), custom_call_target="tpu_custom_call" | custom-call | tf_op jit(solution)/shard_map/pallas_call | solution.py:404
  49.4 0.0 copy-start.1
  49.5 2.3 %copy.11 = bf16[1,4,32,32,128]{4,3,2,1,0:T(8,128)(2,1)} copy(bf16[1,4,32,32,128]{4,3,2,1,0:T(8,128)(2,1)} %get-tuple-element.6) | data formatting | bytes 2097152
  51.8 0.0 copy-done.1
  51.8 0.0 copy-start
  51.8 0.8 %copy.12 = f32[3,3,128,128]{3,2,1,0:T(8,128)} copy(f32[3,3,128,128]{3,2,1,0:T(8,128)S(1)} %copy-done.1) | data formatting | bytes 1179648
  52.6 0.5 copy-done
  53.1 0.8 %copy.13 = f32[3,3,128,128]{3,2,1,0:T(8,128)} copy(f32[3,3,128,128]{3,2,1,0:T(8,128)S(1)} %copy-done) | data formatting | bytes 1179648
Async XLA Ops:
  49.4 2.4 %copy-start.1 = (f32[3,3,128,128]{3,2,1,0:T(8,128)S(1)}, f32[3,3,128,128]{3,2,1,0:T(8,128)}, u32[]{:S(2)}) copy-start(f32[3,3,128,128]{3,2,1,0:T(8,128)} %get-tuple-element.7) | copy-start | bytes 1769476
  51.8 1.3 %copy-start = (f32[3,3,128,128]{3,2,1,0:T(8,128)S(1)}, f32[3,3,128,128]{3,2,1,0:T(8,128)}, u32[]{:S(2)}) copy-start(f32[3,3,128,128]{3,2,1,0:T(8,128)} %get-tuple-element.8) | copy-start | bytes 1769476
where the time goes:
time: 54.5 us; the launch traced here: 53.9 us
  Pallas kernels  48.8 us (90%)
  local copies, waits for them, and re-layouts  4.44 us (8%)
  between operations  0.65 us (1%)
    pallas_call x1, Pallas kernels, block(): pl.pallas_call(functools.partial(kernel, dp_size, space_size, T, S, C, sc...  48.8 us
    unnamed x7, local copies, waits for them, and re-layouts  4.44 us

commit v1 on v0

--- a/solution.py
+++ b/solution.py
@@ -10,7 +10,7 @@
 F32 = jnp.float32
 BF16 = jnp.bfloat16
 MESH = pl.DeviceIdType.MESH
-TRAVEL = (F32, F32, F32, F32)
+TRAVEL = (F32, BF16, BF16, BF16)
 
 
 def plan(dp_size, space_size, rows):
@@ -25,7 +25,7 @@
     dp_size, space_size, tiles, side, chans, scale,
     links, f_ref, c_ref, w1_ref, w2_ref,
     mixed_ref, g1_ref, g2_ref,
-    xc, ac, cc, gc, wb, deriv, agrad, rims, rim_corners,
+    xc, ac, cc, gc, wb, deriv, agrad, rims, rim_corners, turns, picks,
     pool0, pool1, pool2, land0, land1, land2, out0, out1, out2,
     acc1, acc2, ra1, ra2, half1, half2, sb1, sb2, rb1, rb2, sc1, sc2, rc1, rc2, fo1, fo2,
     halo_send, halo_recv, red_send, red_recv,
@@ -88,10 +88,27 @@
         face_lower.append(low)
         face_upper.append(up)
 
-    row_id = lax.broadcasted_iota(jnp.int32, (S, S), 0)
-    col_id = lax.broadcasted_iota(jnp.int32, (S, S), 1)
-    same = (row_id == col_id).astype(F32)
-    turned = (row_id + col_id == S - 1).astype(F32)
+    def blocks(rows, columns, axis, size):
+        at = lax.broadcasted_iota(jnp.int32, (rows, columns), axis)
+        which = sum((at >= k * size).astype(jnp.int32) for k in range(1, 4))
+        return which, at - which * size
+
+    row_side, row_at = blocks(4 * S, 4 * S, 0, S)
+    col_side, col_at = blocks(4 * S, 4 * S, 1, S)
+    alike = row_side == col_side
+    same = jnp.where(alike & (row_at == col_at), 1.0, 0.0)
+    turned = jnp.where(alike & (row_at + col_at == S - 1), 1.0, 0.0)
+    pick_row = lax.broadcasted_iota(jnp.int32, (16, 64), 0)
+    pick_side, pick_at = blocks(16, 64, 1, 16)
+    for t in range(T):
+        flag, corner = jnp.zeros((4 * S, 4 * S), F32), jnp.zeros((16, 64), jnp.int32)
+        for k in range(4):
+            flag = jnp.where(row_side == k, links[t, k, 2].astype(F32), flag)
+            corner = jnp.where(pick_row == k, links[t, k, 4], corner)
+        turns[t] = (flag * turned + (1.0 - flag) * same).astype(BF16)
+        hit = (pick_row == pick_side) & (pick_at == corner)
+        picks[t] = jnp.where(hit, 1.0, 0.0).astype(BF16)
+
     unit_row = lax.broadcasted_iota(jnp.int32, (16, C), 0)
     line_row = lax.broadcasted_iota(jnp.int32, (S, C), 0)
     block_col = lax.broadcasted_iota(jnp.int32, (S, S, C), 1)
@@ -144,16 +161,14 @@
         for place in range(2):
             pool[pl.ds(own_units + place * msg_units, msg_units)] = lands[which][place]
         for t in range(T):
-            for k in range(4):
-                strip = pool[pl.ds(strip_at[t, k], su)].reshape(S, C)
-                flag = links[t, k, 2].astype(F32)
-                turn = (flag * turned + (1.0 - flag) * same).astype(BF16)
-                rims[t, k] = jnp.dot(turn, strip, preferred_element_type=F32)
-                unit = pool[corner_at[t, k]].astype(F32)
-                rim_corners[t, k] = jnp.broadcast_to(
-                    jnp.sum(jnp.where(unit_row == links[t, k, 4], unit, 0.0), 0, keepdims=True),
-                    (8, C),
-                )
+            strips = [pool[pl.ds(strip_at[t, k], su)].reshape(S, C) for k in range(4)]
+            units = [pool[corner_at[t, k]] for k in range(4)]
+            rims[t] = jnp.dot(
+                turns[t], jnp.concatenate(strips, axis=0), preferred_element_type=F32
+            ).reshape(4, S, C)
+            rim_corners[t] = jnp.dot(
+                picks[t], jnp.concatenate(units, axis=0), preferred_element_type=F32
+            )
 
     def shifted(dst, t, at, value, left, right, columns):
         extent = columns.ndim - 2
@@ -167,8 +182,8 @@
     def fill_padded(dst, t, value):
         left, right = rims[t, 3], rims[t, 1]
         shifted(dst, t, pl.ds(1, S), value, left[:, None, :], right[:, None, :], block_col)
-        tl, tr = rim_corners[t, 0, 0:1], rim_corners[t, 1, 0:1]
-        br, bl = rim_corners[t, 2, 0:1], rim_corners[t, 3, 0:1]
+        tl, tr = rim_corners[t, 0:1], rim_corners[t, 1:2]
+        br, bl = rim_corners[t, 2:3], rim_corners[t, 3:4]
         shifted(dst, t, 0, rims[t, 0], tl, tr, line_row)
         shifted(dst, t, S + 1, rims[t, 2], bl, br, line_row)
 
@@ -348,8 +363,8 @@
         agrad[t, S - 1] = agrad[t, S - 1] + rims[t, 2]
         for column, k, above, below in ((0, 3, 0, 3), (S - 1, 1, 1, 2)):
             strip = rims[t, k]
-            strip = strip + jnp.where(line_row == 0, rim_corners[t, above, 0:1], 0.0)
-            strip = strip + jnp.where(line_row == S - 1, rim_corners[t, below, 0:1], 0.0)
+            strip = strip + jnp.where(line_row == 0, rim_corners[t, above : above + 1], 0.0)
+            strip = strip + jnp.where(line_row == S - 1, rim_corners[t, below : below + 1], 0.0)
             agrad[t, :, column : column + 1, :] = (
                 agrad[t, :, column : column + 1, :] + strip[:, None, :]
             )
@@ -376,13 +391,13 @@
 
     pl.loop(0, T // 2)(output)
     second = plane_start(1, second)
-    first = back_start(0, first)
     pl.loop(T // 2, T)(output)
     second = far_start(1, second)
+    first = back_start(0, first)
+    second = back_start(1, second)
     first = pair_back(0, first)
-    second = back_start(1, second)
+    second = pair_back(1, second)
     finish(0, first, g1_ref)
-    second = pair_back(1, second)
     finish(1, second, g2_ref)
     for copy in pending:
         copy.wait_send()
@@ -416,7 +431,9 @@
             vmem((T, S, S, C), F32),
             vmem((T, S, S, C), F32),
             vmem((T, 4, S, C), F32),
-            vmem((T, 4, 8, C), F32),
+            vmem((T, 16, C), F32),
+            vmem((T, 4 * S, 4 * S), BF16),
+            vmem((T, 16, 64), BF16),
         ]
         + [vmem((own_units + 2 * msg_units, 16, C), BF16)] * 3
         + [vmem((2, msg_units, 16, C), BF16)] * 6

time: 54.5 us -> 46 us (0.84)
  Pallas kernels: 48.8 us -> 40.7 us
    pallas_call x1, Pallas kernels: 48.8 us -> 40.7 us  [block(): pl.pallas_call(functools.partial(kernel, dp_size, space_size, T, S, C, sc...]
where the time goes in v1:
time: 46 us; the launch traced here: 45.7 us
  Pallas kernels  40.7 us (88%)
  local copies, waits for them, and re-layouts  4.44 us (10%)
  between operations  0.65 us (1%)
    pallas_call x1, Pallas kernels, block(): pl.pallas_call(functools.partial(kernel, dp_size, space_size, T, S, C, sc...  40.7 us
    unnamed x7, local copies, waits for them, and re-layouts  4.44 us

profile of v1, /device:TPU:0, one launch (start us, length us, event | category | flops | bytes accessed | tf_op | source)
XLA Modules:
  0.0 45.7 jit_solution(2989342543576917097)
XLA Ops:
  0.6 40.7 %shard_map.76 = (bf16[1,4,32,32,128]{4,3,2,1,0:T(8,128)(2,1)}, f32[3,3,128,128]{3,2,1,0:T(8,128)}, f32[3,3,128,128]{3,2,1,0:T(8,128)}) custom-call(s32[4,4,5]{2,1,0:T(4,128)} %links.1, bf16[1,4,32,32,128]{4,3,2,1,0:T(8,128)(2,1)} %f_ref.1, bf16[1,4,32,32,128]{4,3,2,1,0:T(8,128)(2,1)} %c_ref.1, bf16[3,3,128,128]{3,2,1,0:T(8,128)(2,1)} %w1_ref.1, ...), custom_call_target="tpu_custom_call" | custom-call | tf_op jit(solution)/shard_map/pallas_call | solution.py:419
  41.3 0.0 copy-start.1
  41.3 2.3 %copy.11 = bf16[1,4,32,32,128]{4,3,2,1,0:T(8,128)(2,1)} copy(bf16[1,4,32,32,128]{4,3,2,1,0:T(8,128)(2,1)} %get-tuple-element.6) | data formatting | bytes 2097152
  43.6 0.0 copy-done.1
  43.7 0.0 copy-start
  43.7 0.8 %copy.12 = f32[3,3,128,128]{3,2,1,0:T(8,128)} copy(f32[3,3,128,128]{3,2,1,0:T(8,128)S(1)} %copy-done.1) | data formatting | bytes 1179648
  44.5 0.5 %copy-done = f32[3,3,128,128]{3,2,1,0:T(8,128)S(1)} copy-done((f32[3,3,128,128]{3,2,1,0:T(8,128)S(1)}, f32[3,3,128,128]{3,2,1,0:T(8,128)}, u32[]{:S(2)}) %copy-start) | copy-done | bytes 589848
  44.9 0.8 %copy.13 = f32[3,3,128,128]{3,2,1,0:T(8,128)} copy(f32[3,3,128,128]{3,2,1,0:T(8,128)S(1)} %copy-done) | data formatting | bytes 1179648
Async XLA Ops:
  41.3 2.4 %copy-start.1 = (f32[3,3,128,128]{3,2,1,0:T(8,128)S(1)}, f32[3,3,128,128]{3,2,1,0:T(8,128)}, u32[]{:S(2)}) copy-start(f32[3,3,128,128]{3,2,1,0:T(8,128)} %get-tuple-element.7) | copy-start | bytes 1769476
  43.7 1.3 %copy-start = (f32[3,3,128,128]{3,2,1,0:T(8,128)S(1)}, f32[3,3,128,128]{3,2,1,0:T(8,128)}, u32[]{:S(2)}) copy-start(f32[3,3,128,128]{3,2,1,0:T(8,128)} %get-tuple-element.8) | copy-start | bytes 1769476

commit v2 on v1

--- a/solution.py
+++ b/solution.py
@@ -389,9 +389,9 @@
         out = conv(ac, t, w2_ref[...].reshape(9 * C, C), (0, 1, 2)).reshape(S, S, C)
         mixed_ref[0, t] = (f_ref[0, t].astype(F32) + out).astype(BF16)
 
-    pl.loop(0, T // 2)(output)
+    pl.loop(0, 1)(output)
     second = plane_start(1, second)
-    pl.loop(T // 2, T)(output)
+    pl.loop(1, T)(output)
     second = far_start(1, second)
     first = back_start(0, first)
     second = back_start(1, second)

time: 46 us -> 45.4 us (0.987)
  Pallas kernels: 40.7 us -> 40.1 us
    pallas_call x1, Pallas kernels: 40.7 us -> 40.1 us  [block(): pl.pallas_call(functools.partial(kernel, dp_size, space_size, T, S, C, sc...]
where the time goes in v2:
time: 45.4 us; the launch traced here: 45.2 us
  Pallas kernels  40.1 us (88%)
  local copies, waits for them, and re-layouts  4.44 us (10%)
  between operations  0.65 us (1%)
    pallas_call x1, Pallas kernels, block(): pl.pallas_call(functools.partial(kernel, dp_size, space_size, T, S, C, sc...  40.1 us
    unnamed x7, local copies, waits for them, and re-layouts  4.44 us

profile of v2, /device:TPU:0, one launch (start us, length us, event | category | flops | bytes accessed | tf_op | source)
XLA Modules:
  0.0 45.2 jit_solution(5872690830175488102)
XLA Ops:
  0.6 40.1 %shard_map.76 = (bf16[1,4,32,32,128]{4,3,2,1,0:T(8,128)(2,1)}, f32[3,3,128,128]{3,2,1,0:T(8,128)}, f32[3,3,128,128]{3,2,1,0:T(8,128)}) custom-call(s32[4,4,5]{2,1,0:T(4,128)} %links.1, bf16[1,4,32,32,128]{4,3,2,1,0:T(8,128)(2,1)} %f_ref.1, bf16[1,4,32,32,128]{4,3,2,1,0:T(8,128)(2,1)} %c_ref.1, bf16[3,3,128,128]{3,2,1,0:T(8,128)(2,1)} %w1_ref.1, ...), custom_call_target="tpu_custom_call" | custom-call | tf_op jit(solution)/shard_map/pallas_call | solution.py:419
  40.7 0.0 copy-start.1
  40.7 2.3 %copy.11 = bf16[1,4,32,32,128]{4,3,2,1,0:T(8,128)(2,1)} copy(bf16[1,4,32,32,128]{4,3,2,1,0:T(8,128)(2,1)} %get-tuple-element.6) | data formatting | bytes 2097152
  43.1 0.0 copy-done.1
  43.1 0.0 copy-start
  43.1 0.8 %copy.12 = f32[3,3,128,128]{3,2,1,0:T(8,128)} copy(f32[3,3,128,128]{3,2,1,0:T(8,128)S(1)} %copy-done.1) | data formatting | bytes 1179648
  43.9 0.5 %copy-done = f32[3,3,128,128]{3,2,1,0:T(8,128)S(1)} copy-done((f32[3,3,128,128]{3,2,1,0:T(8,128)S(1)}, f32[3,3,128,128]{3,2,1,0:T(8,128)}, u32[]{:S(2)}) %copy-start) | copy-done | bytes 589848
  44.3 0.8 %copy.13 = f32[3,3,128,128]{3,2,1,0:T(8,128)} copy(f32[3,3,128,128]{3,2,1,0:T(8,128)S(1)} %copy-done) | data formatting | bytes 1179648
Async XLA Ops:
  40.7 2.4 %copy-start.1 = (f32[3,3,128,128]{3,2,1,0:T(8,128)S(1)}, f32[3,3,128,128]{3,2,1,0:T(8,128)}, u32[]{:S(2)}) copy-start(f32[3,3,128,128]{3,2,1,0:T(8,128)} %get-tuple-element.7) | copy-start | bytes 1769476
  43.1 1.3 %copy-start = (f32[3,3,128,128]{3,2,1,0:T(8,128)S(1)}, f32[3,3,128,128]{3,2,1,0:T(8,128)}, u32[]{:S(2)}) copy-start(f32[3,3,128,128]{3,2,1,0:T(8,128)} %get-tuple-element.8) | copy-start | bytes 1769476
